TPU v7x, 128 devices: a whole 4x4x4 slice. The times are simulated.
128 devices in a mesh: ep: 32 (over y, z, core), tp: 4 (over x).
Axes of the slice: x: 4, y: 4, z: 4, core: 2. Of those that a mesh axis runs over, the one named last changes fastest.
Arguments:
- queries: bfloat16 [256, 64, 128], P('ep', 'tp'), may hold values from -115 to 115
- key_cache: bfloat16 [256, 4, 1024, 128], P('ep', 'tp'), may hold values from -6 to 6
- stored_value_cache: bfloat16 [256, 4, 1024, 128], P('ep', 'tp'), may hold values from -6 to 6
- new_key: bfloat16 [256, 4, 128], P('ep', 'tp'), may hold values from -4.5 to 4.5
- incoming_value: bfloat16 [256, 4, 128], P('ep', 'tp'), may hold values from -6 to 6
- lengths: int32 [256], P('ep'), may hold values from 1 to 1024, as said below
- policy: int32 [256, 4], P('ep', 'tp'), may hold values from 0 to 2
- retained_blocks: int32 [256, 4, 4], P('ep', 'tp'), may hold values from 0 to 15
- out_weight: bfloat16 [8192, 4096], P(None, 'ep'), may hold values from -0.5 to 0.5
- residual: bfloat16 [256, 4096], P(None, 'ep'), may hold values from -6 to 6
- norm_gain: float32 [4096], replicated, may hold values from 0.1 to 1.9
- routes: int32 [256, 8], replicated, may hold values from 0 to 63, all different within a row; in each aligned block of 256 rows (0 to 255, 256 to 511, ...) at most 64 rows name the same one
- router_logits: float32 [256, 8], replicated, may hold values from -6 to 6
- gate_weight: bfloat16 [64, 4096, 1536], P('ep', None, 'tp'), may hold values from -0.09375 to 0.09375
- up_weight: bfloat16 [64, 4096, 1536], P('ep', None, 'tp'), may hold values from -0.09375 to 0.09375
- down_weight: bfloat16 [64, 1536, 4096], P('ep', 'tp'), may hold values from -0.15625 to 0.15625
Outputs:
- mixed_out: bfloat16 [256, 4096], P(None, ('ep', 'tp'))
Inputs may be any that keep to these rules, and one draw needn't show every extreme that they name: `lengths`: each aligned group of 8 requests holds one of length 1024. At most 64 of all routes name one expert, a bound that some block reaches; a token names 8 different experts.
All inputs are finite; a program needn't handle non-finite values.
Results may differ from a plain program's by a relative error of at most 0.015.
Values may be sent and summed in bfloat16 or wider, within the bound.
A program may use at most 128 MiB of HBM per device.

v0:
```python
import jax
import jax.numpy as jnp
from jax import lax
from jax.sharding import PartitionSpec as P

TOPK = 8
EXP_DEV = 2
BLK = 64
BLOCK_COUNT = 16
WIN = 2
CONTEXT_SLOTS = 1024
CAP = 64
EPSILON = 1e-06


def token_keep(policy, retained_blocks, lengths):
    block_ids = jnp.arange(BLOCK_COUNT, dtype=jnp.int32)
    used_count = (lengths + BLK - 1) // BLK
    used_mask = block_ids < used_count[..., None]
    recent = block_ids >= (used_count - WIN)[..., None]
    last_block = block_ids == (used_count - 1)[..., None]
    listed = jnp.any(retained_blocks[..., :, None] == block_ids, axis=-2)
    policy_col = policy[..., None]
    block_keep = used_mask & (
        (policy_col == 0) & recent | (policy_col == 1) & (listed | last_block) | (policy_col == 2)
    )
    positions = jnp.arange(CONTEXT_SLOTS, dtype=jnp.int32)
    return jnp.repeat(block_keep, BLK, axis=-1) & (positions < lengths[..., None])


def per_device(
    queries,
    key_cache,
    stored_value_cache,
    new_key,
    incoming_value,
    lengths,
    policy,
    retained_blocks,
    out_weight,
    residual,
    norm_gain,
    routes,
    router_logits,
    gate_weight,
    up_weight,
    down_weight,
):
    ep_count = lax.axis_size("ep")
    tp_count = lax.axis_size("tp")
    request_count = queries.shape[0]
    group_heads = queries.shape[1]
    head_size = queries.shape[2]
    head_width = group_heads * head_size
    score_scale = head_size ** (-0.5)
    key_rows = key_cache[:, 0]
    value_rows = stored_value_cache[:, 0]
    own_key = new_key[:, 0]
    own_value = incoming_value[:, 0]
    kept_mask = token_keep(policy[:, 0], retained_blocks[:, 0], lengths)
    own_score = (
        jnp.einsum("rqd,rd->rq", queries, own_key, preferred_element_type=jnp.float32) * score_scale
    )
    scores = (
        jnp.einsum("rqd,rkd->rqk", queries, key_rows, preferred_element_type=jnp.float32)
        * score_scale
    )
    scores = jnp.where(kept_mask[:, None, :], scores, -jnp.inf)
    highest = jnp.maximum(jnp.max(scores, axis=-1), own_score)
    weights = jnp.exp(scores - highest[..., None])
    own_weight = jnp.exp(own_score - highest)
    totals = jnp.sum(weights, axis=-1) + own_weight
    own_low = lax.optimization_barrier(own_weight.astype(jnp.bfloat16)).astype(jnp.float32)
    weighted = jnp.einsum(
        "rqk,rkd->rqd", weights.astype(jnp.bfloat16), value_rows, preferred_element_type=jnp.float32
    )
    weighted = weighted + own_low[..., None] * own_value.astype(jnp.float32)[:, None, :]
    attended = (
        (weighted / totals[..., None]).astype(jnp.bfloat16).reshape(1, request_count, head_width)
    )
    column_count = out_weight.shape[1]
    all_requests = request_count * ep_count
    weight_parts = out_weight.reshape(tp_count, head_width, column_count)
    group_ids = jnp.arange(ep_count, dtype=jnp.int32)
    head_ids = jnp.arange(tp_count, dtype=jnp.int32)
    shard_rows = lax.all_gather(attended, ("ep", "tp"), axis=0, tiled=True)
    device_ids = jnp.arange(shard_rows.shape[0], dtype=jnp.int32)
    terms = jnp.einsum(
        "srk,tkc->strc", shard_rows, weight_parts, preferred_element_type=jnp.float32
    )
    head_match = (device_ids % tp_count)[:, None] == head_ids[None, :]
    chosen = jnp.sum(jnp.where(head_match[:, :, None, None], terms, 0.0), axis=1)
    group_match = (device_ids // tp_count)[:, None] == group_ids[None, :]
    added = jnp.sum(jnp.where(group_match[:, :, None, None], chosen[:, None], 0.0), axis=0)
    projected = added.reshape(all_requests, column_count)
    hidden = (residual.astype(jnp.float32) + projected).astype(jnp.bfloat16)
    experts_all = EXP_DEV * ep_count
    route_flat = routes.reshape(-1)
    onehot = (route_flat[:, None] == jnp.arange(experts_all, dtype=jnp.int32)[None, :]).astype(
        jnp.int32
    )
    route_rank = jnp.sum(jnp.cumsum(onehot, axis=0) * onehot, axis=1) - 1
    slot_index = route_flat * CAP + route_rank
    token_index = jnp.arange(route_flat.shape[0], dtype=jnp.int32) // TOPK
    outgoing_rows = (
        jnp.zeros((experts_all * CAP, column_count), jnp.bfloat16)
        .at[slot_index]
        .set(hidden[token_index])
    )
    arrived = lax.all_to_all(outgoing_rows, "ep", split_axis=0, concat_axis=1, tiled=True)
    rows_float = arrived.astype(jnp.float32)
    normed = (
        rows_float
        * lax.rsqrt(jnp.mean(rows_float * rows_float, axis=-1, keepdims=True) + EPSILON)
        * norm_gain
    ).astype(jnp.bfloat16)
    normed = normed.reshape(EXP_DEV, CAP, normed.shape[1])
    gate = jnp.einsum("ecd,edf->ecf", normed, gate_weight, preferred_element_type=jnp.float32)
    up_proj = jnp.einsum("ecd,edf->ecf", normed, up_weight, preferred_element_type=jnp.float32)
    act = (jax.nn.silu(gate) * up_proj).astype(jnp.bfloat16)
    partial_value = jnp.einsum("ecf,efd->ecd", act, down_weight, preferred_element_type=jnp.float32)
    partial_value = partial_value.reshape(1, EXP_DEV * CAP, partial_value.shape[2])
    returned = lax.all_to_all(
        lax.all_to_all(
            partial_value.astype(jnp.bfloat16), "ep", split_axis=2, concat_axis=1, tiled=True
        ),
        "tp",
        split_axis=2,
        concat_axis=0,
        tiled=True,
    ).astype(partial_value.dtype)
    summed = jnp.sum(returned, axis=0)
    route_weight = jax.nn.softmax(router_logits, axis=-1)
    narrow = summed.shape[1]
    picked_rows = summed[slot_index].reshape(-1, TOPK, narrow)
    mixture = jnp.sum(picked_rows * route_weight[..., None], axis=1)
    tp_index_out = lax.axis_index("tp")
    base_rows = lax.dynamic_slice_in_dim(hidden, tp_index_out * narrow, narrow, 1)
    return (base_rows.astype(jnp.float32) + mixture).astype(jnp.bfloat16)


def solution(mesh):
    return jax.shard_map(
        per_device,
        mesh=mesh,
        in_specs=(
            P("ep", "tp", None),
            P("ep", "tp", None, None),
            P("ep", "tp", None, None),
            P("ep", "tp", None),
            P("ep", "tp", None),
            P("ep"),
            P("ep", "tp"),
            P("ep", "tp", None),
            P(None, "ep"),
            P(None, "ep"),
            P(),
            P(),
            P(),
            P("ep", None, "tp"),
            P("ep", None, "tp"),
            P("ep", "tp", None),
        ),
        out_specs=P(None, ("ep", "tp")),
        check_vma=False,
    )
```

profile of v0, /device:TPU:1, one launch (start us, length us, event | category | flops | bytes accessed | tf_op | source)
XLA Modules:
  0.0 263.7 jit_solution(4339838347839793135)
XLA Ops:
  10.8 2.4 fusion.58
  15.1 18.1 %reduce-window.6 = s32[64,16,128]{2,1,0:T(8,128)S(1)} reduce-window(s32[64,16,128]{2,1,0:T(8,128)S(1)} %fusion.31, s32[]{:T(128)} %constant.89.clone.1), window={size=1x1x128 pad=0_0x0_0x127_0}, to_apply=%region_5.6 | reduce-window | flops 16646144 | bytes 1048580 | tf_op jit(solution)/shard_map/reduce-window
  35.0 50.4 %all-gather.2.cloned.1.call-done = bf16[128,8,2048]{2,1,0:T(8,128)(2,1)} async-done(((bf16[1,8,2048]{2,1,0:T(8,128)(2,1)}), bf16[128,8,2048]{2,1,0:T(8,128)(2,1)}) %all-gather.2.cloned.1.call-update) | async-done | bytes 4194320 | tf_op jit(solution)/shard_map/all_gather | solution.py:86
  85.4 7.0 %select_reduce_fusion.1 = f32[128,8,128]{2,0,1:T(8,128)S(1)} fusion(bf16[4,2048,128,1]{2,1,0,3:T(8,128)(2,1)S(1)} %bitcast.80, bf16[128,8,2048,1]{2,1,0,3:T(8,128)(2,1)} %bitcast.101, pred[128,4]{0,1:T(4,128)(4,1)S(1)} %iota_compare_fusion.8), kind=kOutput, calls=%fused_computation.16 | convolution fusion | flops 2148401152 | bytes 6816256 | tf_op jit(solution)/shard_map/srk,tkc->strc/dot_general | solution.py:88
  92.7 5.6 %select_reduce_fusion = f32[32,8,128]{2,1,0:T(8,128)S(1)} fusion(f32[128,8,128]{2,1,0:T(8,128)S(1)} %copy.111, pred[128,32]{1,0:T(8,128)(4,1)S(1)} %iota_compare_fusion.2), kind=kLoop, calls=%fused_computation.3 | loop fusion | flops 8355840 | bytes 659456 | tf_op jit(solution)/shard_map/reduce_sum | solution.py:94
  98.5 12.9 %scatter_custom_fusion = bf16[4096,128]{1,0:T(8,128)(2,1)} fusion(s32[2048]{0:T(1024)S(1)} %bitcast.94, bf16[256,128]{1,0:T(8,128)(2,1)S(1)} %copy.118, s32[2048]{0:T(1024)S(1)} %broadcast_clamp_fusion.1, bf16[]{:T(256)} %constant.103.clone.1), kind=kCustom, calls=%fused_computation.29 | custom fusion | bytes 1048578 | tf_op jit(solution)/shard_map/scatter | solution.py:108
  111.4 21.7 %all_to_all.40 = bf16[32,128,128]{2,1,0:T(8,128)(2,1)S(1)} all-to-all(bf16[32,128,128]{2,1,0:T(8,128)(2,1)} %bitcast.89), channel_id=1, replica_groups=mesh['ep'=32,'tp'=4] {'ep'}, dimensions={0} | all-to-all | bytes 2097152 | tf_op jit(solution)/shard_map/all_to_all | solution.py:110
  133.3 2.6 copy.119
  135.9 2.7 %reshape.261 = f32[2,64,4096]{2,1,0:T(8,128)} reshape(f32[128,32,128]{2,1,0:T(8,128)} %copy.119) | data formatting | bytes 4194304 | tf_op jit(solution)/shard_map/convert_element_type | solution.py:111
  139.0 4.5 %fusion.34 = f32[2,64,384]{2,1,0:T(8,128)S(1)} fusion(bf16[2,4096,384]{2,1,0:T(8,128)(2,1)} %param.29, f32[2,64,4096]{2,1,0:T(8,128)} %reshape.261, f32[4096]{0:T(1024)S(1)} %copy-done.2, f32[2,64]{1,0:T(2,128)S(1)} %rsqrt.12), kind=kOutput, calls=%fused_computation.38 | convolution fusion | flops 404226048 | bytes 8602112 | tf_op jit(solution)/shard_map/ecd,edf->ecf/dot_general | solution.py:118
  143.6 7.2 %convolution_convert_fusion = bf16[2,64,4096]{2,1,0:T(8,128)(2,1)S(1)} fusion(bf16[2,384,4096]{2,1,0:T(8,128)(2,1)} %param.31, bf16[2,4096,384]{2,1,0:T(8,128)(2,1)} %param.30, f32[2,64,4096]{2,1,0:T(8,128)} %reshape.261, f32[4096]{0:T(1024)S(1)} %copy-done.2, f32[2,64]{1,0:T(2,128)S(1)} %rsqrt.12, f32[2,64,384]{2,1,0:T(8,128)S(1)} %fusion.34), kind=kOutput, calls=%fused_computation.4 | convolution fusion | flops 807698432 | bytes 15942144 | tf_op jit(solution)/shard_map/ecf,efd->ecd/dot_general | solution.py:121
  150.7 3.9 %copy.120 = bf16[1,128,4096]{1,0,2:T(2,128)(2,1)} copy(bf16[1,128,4096]{2,1,0:T(8,128)(2,1)S(1)} %bitcast.85) | data formatting | bytes 2097152 | tf_op jit(solution)/shard_map/convert_element_type | solution.py:125
  155.1 23.4 %reduce.6 = bf16[4096,128]{1,0:T(8,128)(2,1)S(1)} reduce(bf16[4096,1,128]{2,1,0:T(2,128)(2,1)} %bitcast.83, bf16[]{:T(256)} %broadcast.308), dimensions={1}, to_apply=%bitcast.67.reduce_sub_computation | reduce | bytes 2097154
  179.7 20.9 %all_to_all.41 = bf16[32,2,8192]{2,1,0:T(2,128)(2,1)S(1)} all-to-all(bf16[32,2,8192]{2,1,0:T(2,128)(2,1)} %reshape.297), channel_id=1, replica_groups=mesh['ep'=32,'tp'=4] {'ep'}, dimensions={0} | all-to-all | bytes 2097152 | tf_op jit(solution)/shard_map/all_to_all | solution.py:124
  200.6 3.5 %reshape.298 = bf16[4096,1,128]{2,1,0:T(2,128)(2,1)} reshape(bf16[32,2,8192]{2,1,0:T(2,128)(2,1)S(1)} %all_to_all.41) | data formatting | bytes 2097152
  207.1 5.5 %copy.122 = bf16[1,4096,128]{1,0,2:T(2,128)(2,1)} copy(bf16[1,4096,128]{2,1,0:T(8,128)(2,1)} %bitcast.87) | data formatting | bytes 2097152 | tf_op jit(solution)/shard_map/all_to_all | solution.py:124
  212.6 8.4 %reduce.7 = bf16[128,4096]{1,0:T(8,128)(2,1)S(1)} reduce(bf16[128,1,4096]{2,1,0:T(2,128)(2,1)} %bitcast.84, bf16[]{:T(256)} %broadcast.308), dimensions={1}, to_apply=%bitcast.69.reduce_sub_computation | reduce | bytes 2097154
  221.0 2.0 reshape.299
  223.0 3.5 %all-to-all-start.2 = ((bf16[4,2,65536]{2,1,0:T(2,128)(2,1)}), bf16[4,2,65536]{2,1,0:T(2,128)(2,1)S(1)}, u32[]{:S(2)}, u32[]{:S(2)}) async-start(bf16[4,2,65536]{2,1,0:T(2,128)(2,1)} %reshape.299), calls=%async_computation.2 | async-start | bytes 2097152 | tf_op jit(solution)/shard_map/all_to_all | solution.py:123
  226.7 14.8 %all-to-all-done.2 = bf16[4,2,65536]{2,1,0:T(2,128)(2,1)S(1)} async-done(((bf16[4,2,65536]{2,1,0:T(2,128)(2,1)}), bf16[4,2,65536]{2,1,0:T(2,128)(2,1)S(1)}, u32[]{:S(2)}, u32[]{:S(2)}) %all-to-all-start.2) | async-done | bytes 1048608 | tf_op jit(solution)/shard_map/all_to_all | solution.py:123
  241.5 2.3 reshape.300
  243.9 2.7 %copy.123 = bf16[1,4096,128]{1,2,0:T(8,128)(2,1)S(1)} copy(bf16[1,4096,128]{1,0,2:T(2,128)(2,1)} %bitcast.82) | data formatting | bytes 2097152 | tf_op jit(solution)/shard_map/all_to_all | solution.py:123
  246.8 2.0 copy.124
  248.7 7.0 %gather_fusion = f32[2048,32]{1,0:T(8,128)S(1)} fusion(f32[4096,32]{1,0:T(8,128)} %copy.124, s32[2048]{0:T(1024)S(1)} %broadcast_clamp_fusion), kind=kCustom, calls=%fused_computation.1 | custom fusion | bytes 532480 | tf_op jit(solution)/shard_map/gather | solution.py:135
  (74 shorter events, 15.0 us)
Async XLA Ops:
  6.5 78.8 %copy-start = (bf16[8192,128]{1,0:T(8,128)(2,1)S(1)}, bf16[8192,128]{1,0:T(8,128)(2,1)}, u32[]{:S(2)}) copy-start(bf16[8192,128]{1,0:T(8,128)(2,1)} %param.24) | copy-start | bytes 6291460
  6.5 6.9 %copy-start.6 = (bf16[8,1,128]{2,0,1:T(8,128)(2,1)S(1)}, bf16[8,1,128]{2,0,1:T(8,128)(2,1)}, u32[]{:S(2)}) copy-start(bf16[8,1,128]{2,0,1:T(8,128)(2,1)} %param.20) | copy-start | bytes 6148
  6.5 78.8 %all-gather.2.cloned.1.call-start = ((), (), s32[]{:S(2)}) async-start(), calls=%async_computation.3 | async-start | bytes 4227072 | tf_op jit(solution)/shard_map/all_gather | solution.py:86
  9.1 4.4 %copy-start.1 = (bf16[8,1,1024,128]{3,2,1,0:T(8,128)(2,1)S(1)}, bf16[8,1,1024,128]{3,2,1,0:T(8,128)(2,1)}, u32[]{:S(2)}) copy-start(bf16[8,1,1024,128]{3,2,1,0:T(8,128)(2,1)} %param.18) | copy-start | bytes 6291460
  13.2 1.4 copy-start.5
  13.2 1.8 copy-start.4
  135.9 3.1 %copy-start.2 = (f32[4096]{0:T(1024)S(1)}, f32[4096]{0:T(1024)}, u32[]{:S(2)}) copy-start(f32[4096]{0:T(1024)} %param.26) | copy-start | bytes 49156
  220.9 5.5 %copy-start.3 = (f32[256,8]{0,1:T(8,128)S(1)}, f32[256,8]{0,1:T(8,128)}, u32[]{:S(2)}) copy-start(f32[256,8]{0,1:T(8,128)} %param.28) | copy-start | bytes 24580
  223.0 18.6 %all-to-all-start.2 = ((bf16[4,2,65536]{2,1,0:T(2,128)(2,1)}), bf16[4,2,65536]{2,1,0:T(2,128)(2,1)S(1)}, u32[]{:S(2)}, u32[]{:S(2)}) async-start(bf16[4,2,65536]{2,1,0:T(2,128)(2,1)} %reshape.299), calls=%async_computation.2 | async-start | bytes 2097152 | tf_op jit(solution)/shard_map/all_to_all | solution.py:123
Sparse Core Ops, SparseCore 0:
  14.7 70.6 all-gather.1
where the time goes:
time: 265 us; the launch traced here: 264 us
  waiting for transfers between devices  65.3 us (25%)
  other arithmetic  61.5 us (23%)
  local copies, waits for them, and re-layouts  54.8 us (21%)
  blocking collectives  42.5 us (16%)
  matrix products  22.3 us (8%)
  between operations  13.8 us (5%)
  starting transfers between devices  3.52 us (1%)
    all_gather x1, waiting for transfers between devices, per_device(): shard_rows = lax.all_gather(attended, ('ep', 'tp'), axis=0, tiled=True)  50.4 us
    unnamed x2, other arithmetic  31.8 us
    all_to_all x1, blocking collectives, per_device(): lax.all_to_all(outgoing_rows, 'ep', split_axis=0, concat_axis=1, tiled=True)  21.7 us
    all_to_all x1, blocking collectives, per_device(): lax.all_to_all(partial_value.astype(jnp.bfloat16), 'ep', split_axis=2, co...  20.9 us
    another operation x3, other arithmetic  18.5 us
    all_to_all x1, waiting for transfers between devices, per_device(): lax.all_to_all(lax.all_to_all(partial_value.astype(jnp.bfloat16), 'ep', s...  14.8 us
    scatter x1, local copies, waits for them, and re-layouts, per_device(): outgoing_rows = jnp.zeros((experts_all * CAP, column_count), jnp.bfloat16...  12.9 us
    unnamed x22, local copies, waits for them, and re-layouts  11.4 us
  transfers between devices with their start and end apart: 2, of which 2 were waited for; matrix products, arithmetic and copies ran while one was open for 8% of the time, Pallas kernels for 0%

commit v1 on v0

--- a/solution.py
+++ b/solution.py
@@ -11,6 +11,13 @@
 CONTEXT_SLOTS = 1024
 CAP = 64
 EPSILON = 1e-06
+
+
+def swapped_in(array, name, along):
+    size = lax.axis_size(name)
+    blocks = jnp.stack([array for _ in range(size)])
+    blocks = lax.all_to_all(blocks, name, split_axis=0, concat_axis=0)
+    return jnp.concatenate(blocks, axis=along)
 
 
 def token_keep(policy, retained_blocks, lengths):
@@ -83,7 +90,7 @@
     weight_parts = out_weight.reshape(tp_count, head_width, column_count)
     group_ids = jnp.arange(ep_count, dtype=jnp.int32)
     head_ids = jnp.arange(tp_count, dtype=jnp.int32)
-    shard_rows = lax.all_gather(attended, ("ep", "tp"), axis=0, tiled=True)
+    shard_rows = swapped_in(attended, ("ep", "tp"), 0)
     device_ids = jnp.arange(shard_rows.shape[0], dtype=jnp.int32)
     terms = jnp.einsum(
         "srk,tkc->strc", shard_rows, weight_parts, preferred_element_type=jnp.float32

time: 265 us -> 231 us (0.87)
  waiting for transfers between devices: 65.3 us -> 47.6 us
  between operations: 13.8 us -> 0.44 us
  starting transfers between devices: 3.52 us -> 15.5 us
  local copies, waits for them, and re-layouts: 54.8 us -> 45.5 us
    all_gather x1 -> x0, waiting for transfers between devices: 50.4 us -> none  [per_device(): shard_rows = lax.all_gather(attended, ('ep', 'tp'), axis=0, tiled=True)]
    all_to_all x0 -> x1, waiting for transfers between devices: none -> 32.7 us  [swapped_in(): blocks = lax.all_to_all(blocks, name, split_axis=0, concat_axis=0)]
    all_to_all x0 -> x1, starting transfers between devices: none -> 12 us  [swapped_in(): blocks = lax.all_to_all(blocks, name, split_axis=0, concat_axis=0)]
    unnamed x22 -> x25, local copies, waits for them, and re-layouts: 11.4 us -> 5.19 us
  transfers between devices with their start and end apart: 2 -> 2, of which waited for: 2 -> 2; matrix products, arithmetic and copies ran while one was open for 8% -> 9% of each run, Pallas kernels for 0% -> 0%
where the time goes in v1:
time: 231 us; the launch traced here: 230 us
  other arithmetic  59.1 us (26%)
  waiting for transfers between devices  47.6 us (21%)
  local copies, waits for them, and re-layouts  45.5 us (20%)
  blocking collectives  40.6 us (18%)
  matrix products  21.1 us (9%)
  starting transfers between devices  15.5 us (7%)
    all_to_all x1, waiting for transfers between devices, swapped_in(): blocks = lax.all_to_all(blocks, name, split_axis=0, concat_axis=0)  32.7 us
    unnamed x2, other arithmetic  29.4 us
    all_to_all x1, blocking collectives, per_device(): lax.all_to_all(partial_value.astype(jnp.bfloat16), 'ep', split_axis=2, co...  20.7 us
    all_to_all x1, blocking collectives, per_device(): lax.all_to_all(outgoing_rows, 'ep', split_axis=0, concat_axis=1, tiled=True)  20 us
    another operation x3, other arithmetic  18.5 us
    all_to_all x1, waiting for transfers between devices, per_device(): lax.all_to_all(lax.all_to_all(partial_value.astype(jnp.bfloat16), 'ep', s...  14.8 us
    scatter x1, local copies, waits for them, and re-layouts, per_device(): outgoing_rows = jnp.zeros((experts_all * CAP, column_count), jnp.bfloat16...  12.2 us
    all_to_all x1, starting transfers between devices, swapped_in(): blocks = lax.all_to_all(blocks, name, split_axis=0, concat_axis=0)  12 us
  transfers between devices with their start and end apart: 2, of which 2 were waited for; matrix products, arithmetic and copies ran while one was open for 9% of the time, Pallas kernels for 0%

profile of v1, /device:TPU:1, one launch (start us, length us, event | category | flops | bytes accessed | tf_op | source)
XLA Modules:
  0.0 229.8 jit_solution(12641125462949882447)
XLA Ops:
  4.3 2.4 %fusion.62 = (f32[8,16]{1,0:T(8,128)S(1)}, f32[8,16,1024]{2,1,0:T(8,128)S(1)}) fusion(bf16[8,16,128]{2,1,0:T(8,128)(2,1)} %param.16, bf16[8,1,1024,128]{3,2,1,0:T(8,128)(2,1)} %param.17, pred[8,1024]{1,0:T(8,128)(4,1)S(1)} %fusion.47), kind=kOutput, calls=%fused_computation.103 | convolution fusion | flops 33947520 | bytes 2662912 | tf_op jit(solution)/shard_map/rqd,rkd->rqk/dot_general | solution.py:72
  7.4 2.5 %stack.3 = bf16[128,1,8,2048]{3,2,1,0:T(8,128)(2,1)} broadcast(bf16[8,2048]{1,0:T(8,128)(2,1)S(1)} %bitcast.106), dimensions={2,3} | broadcast | bytes 4227072 | tf_op jit(solution)/shard_map/stack | solution.py:18
  9.9 12.0 %all-to-all-start = ((bf16[128,1,8,2048]{3,2,1,0:T(8,128)(2,1)}), bf16[128,1,8,2048]{3,2,1,0:T(8,128)(2,1)}, u32[]{:S(2)}, u32[]{:S(2)}) async-start(bf16[128,1,8,2048]{3,2,1,0:T(8,128)(2,1)} %stack.3), calls=%async_computation | async-start | bytes 8388608 | tf_op jit(solution)/shard_map/all_to_all | solution.py:19
  22.4 18.1 %reduce-window.6 = s32[64,16,128]{2,1,0:T(8,128)S(1)} reduce-window(s32[64,16,128]{2,1,0:T(8,128)S(1)} %fusion.35, s32[]{:T(128)} %constant.89.clone.1), window={size=1x1x128 pad=0_0x0_0x127_0}, to_apply=%region_5.6 | reduce-window | flops 16646144 | bytes 1048580 | tf_op jit(solution)/shard_map/reduce-window
  42.3 32.7 %all-to-all-done = bf16[128,1,8,2048]{3,2,1,0:T(8,128)(2,1)} async-done(((bf16[128,1,8,2048]{3,2,1,0:T(8,128)(2,1)}), bf16[128,1,8,2048]{3,2,1,0:T(8,128)(2,1)}, u32[]{:S(2)}, u32[]{:S(2)}) %all-to-all-start) | async-done | bytes 4194336 | tf_op jit(solution)/shard_map/all_to_all | solution.py:19
  75.0 7.0 %select_reduce_fusion.1 = f32[128,8,128]{2,0,1:T(8,128)S(1)} fusion(bf16[4,2048,128,1]{2,1,0,3:T(8,128)(2,1)S(1)} %bitcast.94, bf16[128,1,8,2048]{3,2,1,0:T(8,128)(2,1)} %all-to-all-done, pred[128,4]{0,1:T(4,128)(4,1)S(1)} %iota_compare_fusion.8), kind=kOutput, calls=%fused_computation.17 | convolution fusion | flops 2148401152 | bytes 6816256 | tf_op jit(solution)/shard_map/srk,tkc->strc/dot_general | solution.py:95
  82.3 5.6 %select_reduce_fusion = f32[32,8,128]{2,1,0:T(8,128)S(1)} fusion(f32[128,8,128]{2,1,0:T(8,128)S(1)} %copy.108, pred[128,32]{1,0:T(8,128)(4,1)S(1)} %iota_compare_fusion.2), kind=kLoop, calls=%fused_computation.3 | loop fusion | flops 8355840 | bytes 659456 | tf_op jit(solution)/shard_map/reduce_sum | solution.py:101
  88.1 12.2 %scatter_custom_fusion = bf16[4096,128]{1,0:T(8,128)(2,1)S(1)} fusion(s32[2048]{0:T(1024)S(1)} %bitcast.109, bf16[256,128]{1,0:T(8,128)(2,1)S(1)} %copy.115, s32[2048]{0:T(1024)S(1)} %broadcast_clamp_fusion.1, bf16[]{:T(256)} %constant.103.clone.1), kind=kCustom, calls=%fused_computation.31 | custom fusion | bytes 1048578 | tf_op jit(solution)/shard_map/scatter | solution.py:115
  100.3 20.0 %all_to_all.45 = bf16[32,128,128]{2,1,0:T(8,128)(2,1)S(1)} all-to-all(bf16[32,128,128]{2,1,0:T(8,128)(2,1)S(1)} %bitcast.103), channel_id=1, replica_groups=mesh['ep'=32,'tp'=4] {'ep'}, dimensions={0} | all-to-all | bytes 2097152 | tf_op jit(solution)/shard_map/all_to_all | solution.py:117
  120.5 2.6 %copy.116 = f32[128,32,128]{2,1,0:T(8,128)} copy(f32[128,32,128]{2,0,1:T(8,128)S(1)} %convert_bitcast_fusion) | data formatting | bytes 4194304 | tf_op jit(solution)/shard_map/convert_element_type | solution.py:118
  123.1 1.8 reshape.265
  125.2 3.9 %fusion.38 = f32[2,64,384]{2,1,0:T(8,128)S(1)} fusion(bf16[2,4096,384]{2,1,0:T(8,128)(2,1)} %param.29, f32[2,64,4096]{2,1,0:T(8,128)S(1)} %reshape.265, f32[4096]{0:T(1024)S(1)} %copy-done.3, f32[2,64]{1,0:T(2,128)S(1)} %rsqrt.12), kind=kOutput, calls=%fused_computation.40 | convolution fusion | flops 404226048 | bytes 8602112 | tf_op jit(solution)/shard_map/ecd,edf->ecf/dot_general | solution.py:125
  129.1 6.6 %convolution_convert_fusion = bf16[2,64,4096]{2,1,0:T(8,128)(2,1)S(1)} fusion(bf16[2,384,4096]{2,1,0:T(8,128)(2,1)} %param.31, bf16[2,4096,384]{2,1,0:T(8,128)(2,1)} %param.30, f32[2,64,4096]{2,1,0:T(8,128)S(1)} %reshape.265, f32[4096]{0:T(1024)S(1)} %copy-done.3, f32[2,64]{1,0:T(2,128)S(1)} %rsqrt.12, f32[2,64,384]{2,1,0:T(8,128)S(1)} %fusion.38), kind=kOutput, calls=%fused_computation.4 | convolution fusion | flops 807698432 | bytes 15942144 | tf_op jit(solution)/shard_map/ecf,efd->ecd/dot_general | solution.py:128
  135.7 2.8 %copy.117 = bf16[1,128,4096]{1,0,2:T(2,128)(2,1)S(1)} copy(bf16[1,128,4096]{2,1,0:T(8,128)(2,1)S(1)} %bitcast.99) | data formatting | bytes 2097152 | tf_op jit(solution)/shard_map/convert_element_type | solution.py:132
  139.1 22.4 %reduce.6 = bf16[4096,128]{1,0:T(8,128)(2,1)S(1)} reduce(bf16[4096,1,128]{2,1,0:T(2,128)(2,1)S(1)} %bitcast.97, bf16[]{:T(256)} %broadcast.310), dimensions={1}, to_apply=%bitcast.80.reduce_sub_computation | reduce | bytes 2097154
  161.7 20.7 %all_to_all.46 = bf16[32,2,8192]{2,1,0:T(2,128)(2,1)S(1)} all-to-all(bf16[32,2,8192]{2,1,0:T(2,128)(2,1)S(1)} %reshape.301), channel_id=1, replica_groups=mesh['ep'=32,'tp'=4] {'ep'}, dimensions={0} | all-to-all | bytes 2097152 | tf_op jit(solution)/shard_map/all_to_all | solution.py:131
  183.6 1.3 copy.118
  184.9 4.7 %copy.119 = bf16[1,4096,128]{1,0,2:T(2,128)(2,1)S(1)} copy(bf16[1,4096,128]{2,1,0:T(8,128)(2,1)} %bitcast.101) | data formatting | bytes 2097152 | tf_op jit(solution)/shard_map/all_to_all | solution.py:131
  189.7 7.0 %reduce.7 = bf16[128,4096]{1,0:T(8,128)(2,1)S(1)} reduce(bf16[128,1,4096]{2,1,0:T(2,128)(2,1)S(1)} %bitcast.98, bf16[]{:T(256)} %broadcast.310), dimensions={1}, to_apply=%bitcast.82.reduce_sub_computation | reduce | bytes 2097154
  196.7 2.0 reshape.303
  198.7 3.5 %all-to-all-start.3 = ((bf16[4,2,65536]{2,1,0:T(2,128)(2,1)}), bf16[4,2,65536]{2,1,0:T(2,128)(2,1)S(1)}, u32[]{:S(2)}, u32[]{:S(2)}) async-start(bf16[4,2,65536]{2,1,0:T(2,128)(2,1)} %reshape.303), calls=%async_computation.3 | async-start | bytes 2097152 | tf_op jit(solution)/shard_map/all_to_all | solution.py:130
  202.4 14.8 %all-to-all-done.3 = bf16[4,2,65536]{2,1,0:T(2,128)(2,1)S(1)} async-done(((bf16[4,2,65536]{2,1,0:T(2,128)(2,1)}), bf16[4,2,65536]{2,1,0:T(2,128)(2,1)S(1)}, u32[]{:S(2)}, u32[]{:S(2)}) %all-to-all-start.3) | async-done | bytes 1048608 | tf_op jit(solution)/shard_map/all_to_all | solution.py:130
  219.6 2.0 copy.121
  221.5 7.2 %gather_fusion = f32[2048,32]{1,0:T(8,128)S(1)} fusion(f32[4096,32]{1,0:T(8,128)} %copy.121, s32[2048]{0:T(1024)S(1)} %broadcast_clamp_fusion), kind=kCustom, calls=%fused_computation.1 | custom fusion | bytes 532480 | tf_op jit(solution)/shard_map/gather | solution.py:142
  (76 shorter events, 13.7 us)
Async XLA Ops:
  0.0 75.0 %copy-start = (bf16[8192,128]{1,0:T(8,128)(2,1)S(1)}, bf16[8192,128]{1,0:T(8,128)(2,1)}, u32[]{:S(2)}) copy-start(bf16[8192,128]{1,0:T(8,128)(2,1)} %param.24) | copy-start | bytes 6291460
  0.0 6.9 %copy-start.7 = (bf16[8,1,128]{2,0,1:T(8,128)(2,1)S(1)}, bf16[8,1,128]{2,0,1:T(8,128)(2,1)}, u32[]{:S(2)}) copy-start(bf16[8,1,128]{2,0,1:T(8,128)(2,1)} %param.20) | copy-start | bytes 6148
  2.5 4.4 %copy-start.2 = (bf16[8,1,1024,128]{3,2,1,0:T(8,128)(2,1)S(1)}, bf16[8,1,1024,128]{3,2,1,0:T(8,128)(2,1)}, u32[]{:S(2)}) copy-start(bf16[8,1,1024,128]{3,2,1,0:T(8,128)(2,1)} %param.18) | copy-start | bytes 6291460
  9.9 12.0 %copy-start.6 = (s32[256,8]{0,1:T(8,128)S(1)}, s32[256,8]{0,1:T(8,128)}, u32[]{:S(2)}) copy-start(s32[256,8]{0,1:T(8,128)} %param.27) | copy-start | bytes 24580
  9.9 12.3 %copy-start.5 = (bf16[256,128]{1,0:T(8,128)(2,1)S(1)}, bf16[256,128]{1,0:T(8,128)(2,1)}, u32[]{:S(2)}) copy-start(bf16[256,128]{1,0:T(8,128)(2,1)} %param.25) | copy-start | bytes 196612
  9.9 65.1 %all-to-all-start = ((bf16[128,1,8,2048]{3,2,1,0:T(8,128)(2,1)}), bf16[128,1,8,2048]{3,2,1,0:T(8,128)(2,1)}, u32[]{:S(2)}, u32[]{:S(2)}) async-start(bf16[128,1,8,2048]{3,2,1,0:T(8,128)(2,1)} %stack.3), calls=%async_computation | async-start | bytes 8388608 | tf_op jit(solution)/shard_map/all_to_all | solution.py:19
  123.1 2.2 copy-start.3
  196.7 5.5 %copy-start.4 = (f32[256,8]{0,1:T(8,128)S(1)}, f32[256,8]{0,1:T(8,128)}, u32[]{:S(2)}) copy-start(f32[256,8]{0,1:T(8,128)} %param.28) | copy-start | bytes 24580
  198.7 18.6 %all-to-all-start.3 = ((bf16[4,2,65536]{2,1,0:T(2,128)(2,1)}), bf16[4,2,65536]{2,1,0:T(2,128)(2,1)S(1)}, u32[]{:S(2)}, u32[]{:S(2)}) async-start(bf16[4,2,65536]{2,1,0:T(2,128)(2,1)} %reshape.303), calls=%async_computation.3 | async-start | bytes 2097152 | tf_op jit(solution)/shard_map/all_to_all | solution.py:130
  221.5 8.3 %copy-start.1 = (bf16[8192,128]{1,0:T(8,128)(2,1)S(1)}, bf16[8192,128]{1,0:T(8,128)(2,1)}, u32[]{:S(2)}) copy-start(bf16[8192,128]{1,0:T(8,128)(2,1)} %param.24) | copy-start | bytes 6291460
